TPU v7x, 512 devices: a whole 4x8x8 slice. The times are simulated.
512 devices in a mesh: wide: 32 (over z, x), narrow: 16 (over y, core).
Axes of the slice: x: 4, y: 8, z: 8, core: 2. Of those that a mesh axis runs over, the one named last changes fastest.
Arguments:
- embeddings: bfloat16 [262144, 1024], P(('wide', 'narrow')), may hold values from -32 to 32
- valid: int32 [262144], P(('wide', 'narrow')), may hold values from 0 to 1, as said below
Outputs:
- whitened: bfloat16 [262144, 1024], P(('wide', 'narrow'))
Inputs may be any that keep to these rules, and one draw needn't show every extreme that they name: The first row of every aligned block of 16 rows has valid = 1.
All inputs are finite; a program needn't handle non-finite values.
Results may differ from a plain program's by a relative error of at most 0.001.
Values sent between devices are 32-bit elements; how exact they have to be, the bound alone decides.
A program may use at most 64 MiB of HBM per device.

v0:
```python
import jax
import jax.numpy as jnp
from jax import lax
from jax.sharding import PartitionSpec as P


def merged(part, axis, combine):
    gathered = jax.tree.map(lambda a: lax.all_gather(a, axis), part)

    def take(source):
        return jax.tree.map(lambda a: lax.dynamic_index_in_dim(a, source, 0, False), gathered)

    return lax.fori_loop(
        1, lax.axis_size(axis), lambda source, state: combine(state, take(source)), take(0)
    )


def shifted_scatter(gram, count_local, sums_local, center):
    return (
        gram
        - sums_local[:, None] * center[None, :]
        - center[:, None] * sums_local[None, :]
        + count_local * center[:, None] * center[None, :]
    )


def narrow_rows(term):
    return lax.psum_scatter(term, "narrow", scatter_dimension=0, tiled=True)


def on_device(embeddings, valid):
    width = embeddings.shape[1]
    narrow_count = lax.axis_size("narrow")
    row_span = width // narrow_count
    offset = lax.axis_index("narrow") * row_span
    mask_half = valid.astype(jnp.bfloat16)
    count_local = jnp.sum(valid.astype(jnp.float32))
    masked = embeddings * mask_half[:, None]
    gram = lax.dot_general(
        masked, embeddings, (((0,), (0,)), ((), ())), preferred_element_type=jnp.float32
    )
    sums_local = jnp.dot(mask_half[None, :], embeddings, preferred_element_type=jnp.float32)[0]
    group_count, group_sums = lax.psum((count_local, sums_local), "narrow")
    group_center = group_sums / group_count
    term = shifted_scatter(gram, count_local, sums_local, group_center)
    group_rows = narrow_rows(term)

    def pooled(left, right):
        left_count, left_sums, left_rows = left
        right_count, right_sums, right_rows = right
        joined = left_count + right_count
        shifts = left_sums / left_count - right_sums / right_count
        shift_rows = lax.dynamic_slice_in_dim(shifts, offset, row_span, 0)
        extra = left_count * right_count / joined * shift_rows[:, None] * shifts[None, :]
        return (joined, left_sums + right_sums, left_rows + right_rows + extra)

    count, sums, own_rows = merged((group_count, group_sums, group_rows), "wide", pooled)
    center = sums / count
    cov_rows = own_rows / count
    ident_rows = (
        lax.broadcasted_iota(jnp.int32, (row_span, width), 0) + offset
        == lax.broadcasted_iota(jnp.int32, (row_span, width), 1)
    ).astype(jnp.float32)
    diag_block = lax.dynamic_slice_in_dim(cov_rows, offset, row_span, 1)
    trace_part = jnp.sum(jnp.diagonal(diag_block))
    square_part = jnp.sum(cov_rows * cov_rows)
    trace_cov, square_sum = lax.psum((trace_part, square_part), "narrow")
    ridge_add = 0.05 * trace_cov / width + 1e-06
    norm_frob = jnp.sqrt(square_sum + 2.0 * ridge_add * trace_cov + width * ridge_add * ridge_add)
    base_rows = (cov_rows + ridge_add * ident_rows) / norm_frob
    root_rows = (3.0 * ident_rows - base_rows) / 2.0
    root_full = lax.all_gather(root_rows, "narrow", axis=0, tiled=True)
    first = jnp.dot(
        base_rows, root_full, precision=lax.Precision.HIGHEST, preferred_element_type=jnp.float32
    )
    second = jnp.dot(
        first, root_full, precision=lax.Precision.HIGHEST, preferred_element_type=jnp.float32
    )
    factor = (3.0 * ident_rows - second) / 2.0
    root_rows = jnp.dot(
        factor, root_full, precision=lax.Precision.HIGHEST, preferred_element_type=jnp.float32
    )
    centered_x = embeddings.astype(jnp.float32) - center
    product = jnp.dot(
        centered_x,
        lax.all_gather(root_rows, "narrow", axis=0, tiled=True),
        precision=lax.Precision.HIGHEST,
        preferred_element_type=jnp.float32,
    )
    return (product / jnp.sqrt(norm_frob)).astype(jnp.bfloat16)


def solution(mesh):
    in_specs = (P(("wide", "narrow"), None), P(("wide", "narrow")))
    out_specs = P(("wide", "narrow"), None)
    return jax.shard_map(
        on_device, mesh=mesh, in_specs=in_specs, out_specs=out_specs, check_vma=False
    )
```

profile of v0, /device:TPU:1, one launch (start us, length us, event | category | flops | bytes accessed | tf_op | source)
XLA Modules:
  0.0 490.2 jit_solution(10090267257957100686)
XLA Ops:
  7.2 1.3 convert_reduce_fusion
  8.5 1.5 fusion.12
  10.0 30.9 %all-reduce.2 = (f32[]{:T(128)}, f32[1024]{0:T(1024)S(1)}) all-reduce(f32[]{:T(128)} %convert_reduce_fusion, f32[1024]{0:T(1024)S(1)} %bitcast.31), channel_id=1, replica_groups=mesh['wide'=32,'narrow'=16] {'narrow'}, use_global_device_ids=true, to_apply=%region_1.0 | all-reduce | flops 1025 | bytes 8200 | tf_op jit(solution)/shard_map/psum | solution.py:43
  40.8 1.3 broadcast_multiply_fusion
  42.1 5.4 %multiply_add_fusion = f32[1024,1024]{1,0:T(8,128)} fusion(bf16[512,1024]{1,0:T(8,128)(2,1)} %param.4, f32[1024]{0:T(1024)S(1)} %get-tuple-element.284, f32[1024]{0:T(1024)S(1)} %bitcast.32, f32[1024]{0:T(1024)S(1)} %get-tuple-element.285, bf16[512]{0:T(512)(128)(2,1)S(1)} %convert_element_type.15), kind=kOutput, calls=%fused_computation.6 | convolution fusion | flops 1080557568 | bytes 5256192 | tf_op jit(solution)/shard_map/dot_general | solution.py:39
  47.6 62.6 %reduce-scatter.2.cloned.1.call-done = f32[64,1024]{1,0:T(8,128)} async-done(((f32[1024,1024]{1,0:T(8,128)}), f32[64,1024]{1,0:T(8,128)}) %reduce-scatter.2.cloned.1.call-update) | async-done | bytes 262160 | tf_op jit(solution)/shard_map/reduce_scatter | solution.py:28
  110.2 35.0 %all-gather = f32[32768]{0:T(1024)S(1)} all-gather(f32[1024]{0:T(1024)S(1)} %get-tuple-element.281), channel_id=2, replica_groups=mesh['wide'=32,'narrow'=16] {'wide'}, dimensions={0}, use_global_device_ids=true | all-gather | bytes 135168 | tf_op jit(solution)/shard_map/all_gather | solution.py:8
  145.3 1.3 dynamic-slice
  146.6 1.3 dynamic-update-slice
  147.9 59.3 %all-reduce = f32[32]{0:T(128)S(1)} all-reduce(f32[32]{0:T(128)S(1)} %dynamic-update-slice), channel_id=1, replica_groups=mesh['wide'=32,'narrow'=16] {'wide'}, use_global_device_ids=true, to_apply=%add | all-reduce | flops 32 | bytes 256
  207.2 11.9 %all-gather.10.cloned.1.call-done = f32[2048,1024]{1,0:T(8,128)} async-done(((f32[64,1024]{1,0:T(8,128)}), f32[2048,1024]{1,0:T(8,128)}) %all-gather.10.cloned.1.call-update) | async-done | bytes 8388624 | tf_op jit(solution)/shard_map/all_gather | solution.py:8
  220.1 116.4 %while.21 = (s32[]{:T(128)}, f32[]{:T(128)}, f32[1024]{0:T(1024)S(1)}, f32[64,1024]{1,0:T(8,128)S(1)}, f32[32]{0:T(128)S(1)}, /*index=5*/f32[32,1024]{1,0:T(8,12...) while((s32[]{:T(128)}, f32[]{:T(128)}, f32[1024]{0:T(1024)S(1)}, ...), condition=%wide.region_5.6_spmd, body=%wide.region_4.5_spmd.sunk | while | flops 200776 | bytes 816103 | solution.py:13
  226.6 1.0 fusion.24
  245.3 1.0 fusion.24
  260.3 1.0 fusion.24
  264.1 1.0 fusion.24
  279.1 1.0 fusion.24
  338.7 37.7 %all-reduce.1 = (f32[]{:T(128)}, f32[]{:T(128)}) all-reduce(f32[]{:T(128)} %get-tuple-element.282, f32[]{:T(128)} %reduce_sum.28), channel_id=1, replica_groups=mesh['wide'=32,'narrow'=16] {'narrow'}, use_global_device_ids=true, to_apply=%region_9.10 | all-reduce | flops 2 | bytes 16 | tf_op jit(solution)/shard_map/psum | solution.py:67
  379.6 39.5 %all-gather.6.cloned.1.call-done = f32[1024,1024]{1,0:T(8,128)} async-done(((f32[64,1024]{1,0:T(8,128)}), f32[1024,1024]{1,0:T(8,128)}) %all-gather.6.cloned.1.call-update) | async-done | bytes 4194320 | tf_op jit(solution)/shard_map/all_gather | solution.py:72
  419.1 5.0 %fusion.11 = f32[64,1024]{1,0:T(8,128)S(1)} fusion(f32[1024,1024]{1,0:T(8,128)} %all-gather.6.cloned.1.call-done, f32[64,1024]{1,0:T(8,128)S(1)} %get-tuple-element.283, f32[]{:T(128)S(6)} %sqrt.6, f32[]{:T(128)S(6)} %add.145, s32[64]{0:T(128)S(1)} %iota_add_fusion), kind=kOutput, calls=%fused_computation.29 | convolution fusion | flops 805568512 | bytes 4718856 | tf_op jit(solution)/shard_map/dot_general | solution.py:73
  424.2 2.7 fusion.7
  426.8 3.4 fusion.13
  430.2 43.9 %all-gather.8.cloned.1.call-done = f32[1024,1024]{1,0:T(8,128)} async-done(((f32[64,1024]{1,0:T(8,128)}), f32[1024,1024]{1,0:T(8,128)}) %all-gather.8.cloned.1.call-update) | async-done | bytes 4194320 | tf_op jit(solution)/shard_map/all_gather | solution.py:86
  474.1 9.6 %divide_convert_fusion = bf16[512,1024]{1,0:T(8,128)(2,1)} fusion(f32[1024,1024]{1,0:T(8,128)} %all-gather.8.cloned.1.call-done, bf16[512,1024]{1,0:T(8,128)(2,1)S(1)} %copy-done.1, f32[]{:T(128)S(6)} %sqrt.7, f32[1024]{0:T(1024)S(1)} %broadcast_divide_fusion.1), kind=kOutput, calls=%fused_computation.7 | convolution fusion | flops 6444548096 | bytes 6295556 | tf_op jit(solution)/shard_map/dot_general | solution.py:84
  (176 shorter events, 73.6 us)
Async XLA Ops:
  6.5 103.6 %reduce-scatter.2.cloned.1.call-start = ((), (), s32[]{:S(2)}) async-start(), calls=%async_computation.1 | async-start | bytes 4456448 | tf_op jit(solution)/shard_map/reduce_scatter | solution.py:28
  47.5 171.6 %all-gather.10.cloned.1.call-start = ((), (), s32[]{:S(2)}) async-start(), calls=%async_computation.4 | async-start | bytes 8650752 | tf_op jit(solution)/shard_map/all_gather | solution.py:8
  110.2 308.9 %all-gather.6.cloned.1.call-start = ((), (), s32[]{:S(2)}) async-start(), calls=%async_computation.2 | async-start | bytes 4456448 | tf_op jit(solution)/shard_map/all_gather | solution.py:72
  379.4 94.7 %all-gather.8.cloned.1.call-start = ((), (), s32[]{:S(2)}) async-start(), calls=%async_computation.3 | async-start | bytes 4456448 | tf_op jit(solution)/shard_map/all_gather | solution.py:86
  419.1 5.0 %copy-start = (f32[1024,1024]{1,0:T(8,128)S(1)}, f32[1024,1024]{1,0:T(8,128)}, u32[]{:S(2)}) copy-start(f32[1024,1024]{1,0:T(8,128)} %all-gather.6.cloned.1.call-done) | copy-start | bytes 12582916
  424.1 50.0 %copy-start.1 = (bf16[512,1024]{1,0:T(8,128)(2,1)S(1)}, bf16[512,1024]{1,0:T(8,128)(2,1)}, u32[]{:S(2)}) copy-start(bf16[512,1024]{1,0:T(8,128)(2,1)} %param.4) | copy-start | bytes 3145732
Sparse Core Ops, SparseCore 0:
  47.6 62.4 reduce-scatter.1
  113.3 105.7 all-gather.9
  379.5 39.5 all-gather.5
  430.3 43.7 all-gather.7
where the time goes:
time: 494 us; the launch traced here: 490 us
  blocking collectives  163 us (33%)
  waiting for transfers between devices  158 us (32%)
  other arithmetic  60.5 us (12%)
  loops' own time  42.7 us (9%)
  matrix products  27.4 us (6%)
  local copies, waits for them, and re-layouts  23.1 us (5%)
  between operations  15.4 us (3%)
    reduce_scatter x1, waiting for transfers between devices, narrow_rows(): return lax.psum_scatter(term, 'narrow', scatter_dimension=0, tiled=True)  62.6 us
    unnamed x1, blocking collectives  59.3 us
    all_gather x1, waiting for transfers between devices, on_device(): lax.all_gather(root_rows, 'narrow', axis=0, tiled=True)  43.9 us
    another operation x1, loops' own time, merged(): lax.fori_loop(1, lax.axis_size(axis), lambda source, state: combine(state...  42.7 us
    all_gather x1, waiting for transfers between devices, on_device(): root_full = lax.all_gather(root_rows, 'narrow', axis=0, tiled=True)  39.5 us
    psum x1, blocking collectives, on_device(): trace_cov, square_sum = lax.psum((trace_part, square_part), 'narrow')  37.7 us
    all_gather x1, blocking collectives, merged(): gathered = jax.tree.map(lambda a: lax.all_gather(a, axis), part)  35 us
    add x31, other arithmetic, pooled(): return (joined, left_sums + right_sums, left_rows + right_rows + extra)  32.3 us
  transfers between devices with their start and end apart: 4, of which 4 were waited for; matrix products, arithmetic and copies ran while one was open for 1% of the time, Pallas kernels for 0%

commit v1 on v0

v1 whole, which is shorter than its diff:
```python
import functools

import jax
import jax.numpy as jnp
from jax import lax
from jax.experimental import pallas as pl
from jax.experimental.pallas import tpu as pltpu
from jax.sharding import PartitionSpec as P

MESH = pl.DeviceIdType.MESH
F32 = jnp.float32
BF16 = jnp.bfloat16

SIZE = {"z": 8, "x": 4, "y": 8, "c": 2}
BLK = 128
NB = 8
HALF_ROWS = ((0, 3, 4, 7), (1, 2, 5, 6))
A1X, A2X = 256, 192
AX = A1X + A2X
A1P, A2P = A1X // 8, A2X // 8
B0 = 4 * AX
C0 = B0 + 256
D0 = C0 + 256
HALF = D0 + 8
FAR_8 = (4, 3, 5, 2, 6, 1, 7)
FAR_4 = (2, 1, 3)


def block_place(i, j):
    half = 0 if i in HALF_ROWS[0] else 1
    row = 0
    for k in HALF_ROWS[half]:
        if k == i:
            break
        row += NB - k
    return half, (row + j - i) * BLK


def coords():
    w, n = lax.axis_index("wide"), lax.axis_index("narrow")
    return {"z": w // 4, "x": w % 4, "y": n // 2, "c": n % 2}


def moved(me, axis, step):
    at = dict(me)
    at[axis] = lax.rem(me[axis] + step + SIZE[axis], SIZE[axis])
    return at


def ident(at):
    return (at["z"] * 4 + at["x"], at["y"] * 2 + at["c"])


def order(axis):
    return {"x": FAR_4, "y": FAR_8, "z": FAR_8, "c": (1,)}[axis]


def rows(start, size):
    return pl.ds(pl.multiple_of(start, 8), size)


def pool_kernel(
    x_ref, valid_ref, out_ref,
    g, got, acc,
    r1a, r1b, r1c, r1d, s1a, s1b, s1c, s1d,
    r2a, r2e, r2b, r2c, r2d, s2a, s2e, s2b, s2c, s2d,
    r3a, r3e, r3b, r3c, r3d,
    send_sem, recv_sem,
):
    me = coords()
    core = me["c"]
    barrier = pltpu.get_barrier_semaphore()
    count = 0
    for axis in ("z", "y", "x", "c"):
        for step in order(axis):
            pl.semaphore_signal(
                barrier, inc=1, device_id=ident(moved(me, axis, step)), device_id_type=MESH
            )
            count += 1

    mask = valid_ref[...].astype(F32)
    mask_half = mask.astype(BF16)
    for half in range(2):
        for i in HALF_ROWS[half]:
            left = x_ref[:, i * BLK:(i + 1) * BLK].T * mask_half
            panel = jnp.dot(left, x_ref[:, i * BLK:], preferred_element_type=F32)
            for j in range(i, NB):
                _, row = block_place(i, j)
                g[half, row:row + BLK, :] = panel[:, (j - i) * BLK:(j - i + 1) * BLK]
    sums = jnp.dot(
        jnp.broadcast_to(mask_half, (16, mask.shape[1])), x_ref[...], preferred_element_type=F32
    )
    for i in range(NB):
        g[0, D0 + i:D0 + i + 1, :] = sums[0:1, i * BLK:(i + 1) * BLK]
    g[1, D0:D0 + 8, :] = jnp.broadcast_to(jnp.sum(mask, axis=1, keepdims=True), (8, BLK))

    pl.semaphore_wait(barrier, count)

    used = []

    def copy(src, dst, axis, step):
        at = len(used)
        made = pltpu.make_async_remote_copy(
            src_ref=src, dst_ref=dst, send_sem=send_sem.at[at], recv_sem=recv_sem.at[at],
            device_id=ident(moved(me, axis, step)), device_id_type=MESH,
        )
        used.append(made)
        made.start()
        return made

    def arrive(copies):
        for made in copies:
            made.wait_recv()

    cuts = [(B0, HALF - B0)] + [(j * AX, AX) for j in range(4)]
    pair = [
        copy(g.at[1 - core, pl.ds(start, size)], got.at[pl.ds(start, size)], "c", 1)
        for start, size in cuts
    ]
    pair[0].wait_recv()
    acc[B0:HALF, :] = g[core, B0:HALF, :] + got[B0:HALF, :]
    w1b = [copy(acc.at[rows(B0 + 32 * moved(me, "y", s)["y"], 32)], r1b.at[s - 1], "y", s) for s in FAR_8]
    w1c = [copy(acc.at[rows(C0 + 32 * moved(me, "z", s)["z"], 32)], r1c.at[s - 1], "z", s) for s in FAR_8]
    w1d = [copy(acc.at[pl.ds(D0, 8)], r1d.at[s - 1], "x", s) for s in FAR_4]
    arrive(pair[1:])
    acc[0:B0, :] = g[core, 0:B0, :] + got[0:B0, :]
    w1a = [copy(acc.at[rows(AX * moved(me, "x", s)["x"], AX)], r1a.at[s - 1], "x", s) for s in FAR_4]

    def total(own, parts, n):
        value = own
        for k in range(n):
            value = value + parts[k]
        return value

    arrive(w1d)
    s1d[...] = total(acc[D0:HALF, :], r1d, 3)
    w2d = [copy(s1d, r2d.at[s - 1], "y", s) for s in FAR_8]
    arrive(w1a)
    s1a[...] = total(acc[rows(AX * me["x"], AX), :], r1a, 3)
    w2a = [copy(s1a.at[rows(A1P * moved(me, "y", s)["y"], A1P)], r2a.at[s - 1], "y", s) for s in FAR_8]
    w2e = [copy(s1a.at[rows(A1X + A2P * moved(me, "z", s)["z"], A2P)], r2e.at[s - 1], "z", s) for s in FAR_8]
    arrive(w1b)
    s1b[...] = total(acc[rows(B0 + 32 * me["y"], 32), :], r1b, 7)
    w2b = [copy(s1b.at[rows(8 * moved(me, "x", s)["x"], 8)], r2b.at[s - 1], "x", s) for s in FAR_4]
    arrive(w1c)
    s1c[...] = total(acc[rows(C0 + 32 * me["z"], 32), :], r1c, 7)
    w2c = [copy(s1c.at[rows(8 * moved(me, "x", s)["x"], 8)], r2c.at[s - 1], "x", s) for s in FAR_4]

    arrive(w2d)
    s2d[...] = total(s1d[...], r2d, 7)
    w3d = [copy(s2d, r3d.at[s - 1], "z", s) for s in FAR_8]
    arrive(w2a)
    s2a[...] = total(s1a[rows(A1P * me["y"], A1P), :], r2a, 7)
    w3a = [copy(s2a, r3a.at[s - 1], "z", s) for s in FAR_8]
    arrive(w2e)
    s2e[...] = total(s1a[rows(A1X + A2P * me["z"], A2P), :], r2e, 7)
    w3e = [copy(s2e, r3e.at[s - 1], "y", s) for s in FAR_8]
    arrive(w2b)
    s2b[...] = total(s1b[rows(8 * me["x"], 8), :], r2b, 3)
    w3b = [copy(s2b, r3b.at[s - 1], "z", s) for s in FAR_8]
    arrive(w2c)
    s2c[...] = total(s1c[rows(8 * me["x"], 8), :], r2c, 3)
    w3c = [copy(s2c, r3c.at[s - 1], "y", s) for s in FAR_8]

    def share(start, size, axis):
        piece = out_ref.at[core, rows(start, size)]
        return [copy(piece, piece, axis, s) for s in order(axis)]

    ax = AX * me["x"]
    a_at, e_at = ax + A1P * me["y"], ax + A1X + A2P * me["z"]
    b_at, c_at = B0 + 32 * me["y"] + 8 * me["x"], C0 + 32 * me["z"] + 8 * me["x"]
    arrive(w3d)
    out_ref[core, D0:HALF, :] = total(s2d[...], r3d, 7)
    w6 = share(D0, 8, "c")
    arrive(w3a)
    out_ref[core, rows(a_at, A1P), :] = total(s2a[...], r3a, 7)
    w4a = share(a_at, A1P, "y")
    arrive(w3e)
    out_ref[core, rows(e_at, A2P), :] = total(s2e[...], r3e, 7)
    w4e = share(e_at, A2P, "z")
    arrive(w3b)
    out_ref[core, rows(b_at, 8), :] = total(s2b[...], r3b, 7)
    w4b = share(b_at, 8, "x")
    arrive(w3c)
    out_ref[core, rows(c_at, 8), :] = total(s2c[...], r3c, 7)
    w4c = share(c_at, 8, "x")

    arrive(w4b)
    w5b = share(B0 + 32 * me["y"], 32, "y")
    arrive(w4c)
    w5c = share(C0 + 32 * me["z"], 32, "z")
    arrive(w4a)
    w5a = share(ax, A1X, "x")
    arrive(w4e)
    w5e = share(ax + A1X, A2X, "x")
    w6 += share(ax, AX, "c")
    for k, s in enumerate(FAR_4):
        w5a[k].wait_recv()
        w5e[k].wait_recv()
        w6 += share(AX * moved(me, "x", -s)["x"], AX, "c")
    arrive(w5b)
    w6 += share(B0, 256, "c")
    arrive(w5c)
    w6 += share(C0, 256, "c")
    arrive(w6)
    for made in used:
        made.wait_send()


N_COPIES = 5 + 7 + 7 + 3 + 3 + 7 * 3 + 3 * 2 + 7 * 5 + 7 * 2 + 3 * 2 + 7 * 2 + 3 * 2 + 7


def pool(x, valid):
    part = lambda n, r: pltpu.VMEM((n, r, BLK), F32)
    flat = lambda r: pltpu.VMEM((r, BLK), F32)
    whole = pl.BlockSpec(memory_space=pltpu.VMEM)
    return pl.pallas_call(
        pool_kernel,
        name="pool",
        out_shape=jax.ShapeDtypeStruct((2, HALF, BLK), F32),
        in_specs=[whole, whole],
        out_specs=whole,
        scratch_shapes=[
            part(2, HALF), flat(HALF), flat(HALF),
            part(3, AX), part(7, 32), part(7, 32), part(3, 8), flat(AX), flat(32), flat(32), flat(8),
            part(7, A1P), part(7, A2P), part(3, 8), part(3, 8), part(7, 8),
            flat(A1P), flat(A2P), flat(8), flat(8), flat(8),
            part(7, A1P), part(7, A2P), part(7, 8), part(7, 8), part(7, 8),
            pltpu.SemaphoreType.DMA((N_COPIES,)), pltpu.SemaphoreType.DMA((N_COPIES,)),
        ],
        compiler_params=pltpu.CompilerParams(
            collective_id=0, has_side_effects=True, vmem_limit_bytes=40 * 2**20
        ),
    )(x, valid)


def split(value):
    high = value.astype(BF16)
    return high, (value - high.astype(F32)).astype(BF16)


def white_kernel(f_ref, x_ref, o_ref, b, b2, bh, bl, ph, pp, qh, ql):
    width = NB * BLK
    count = f_ref[1, D0:D0 + 1, :]
    inverse = 1.0 / count
    sums = f_ref[0, D0:D0 + 8, :]
    center = sums / count
    diag = (
        lax.broadcasted_iota(jnp.int32, (BLK, BLK), 0)
        == lax.broadcasted_iota(jnp.int32, (BLK, BLK), 1)
    )
    eye = diag.astype(F32)

    def at(i):
        return slice(i * BLK, (i + 1) * BLK)

    trace = jnp.zeros((BLK, BLK), F32)
    square = jnp.zeros((BLK, BLK), F32)
    for i in range(NB):
        column = jnp.broadcast_to(sums[i:i + 1, :], (BLK, BLK)).T
        for j in range(i, NB):
            half, row = block_place(i, j)
            scatter = f_ref[half, row:row + BLK, :] - column * center[j:j + 1, :]
            cov = scatter * inverse
            if i == j:
                trace = trace + jnp.where(diag, cov, 0.0)
                square = square + cov * cov
            else:
                square = square + 2.0 * (cov * cov)
            b[at(i), at(j)] = cov
    trace = jnp.sum(trace, axis=(0, 1), keepdims=True)
    square = jnp.sum(square, axis=(0, 1), keepdims=True)
    ridge = 0.05 * trace / width + 1e-06
    norm = jnp.sqrt(square + 2.0 * ridge * trace + width * ridge * ridge)
    inv_norm = 1.0 / norm

    def put(value, i, j, high, low):
        h, l = split(value)
        high[at(i), at(j)] = h
        low[at(i), at(j)] = l
        if i != j:
            h, l = split(value.T)
            high[at(j), at(i)] = h
            low[at(j), at(i)] = l

    for i in range(NB):
        for j in range(i, NB):
            value = b[at(i), at(j)]
            if i == j:
                value = value + ridge * eye
            value = value * inv_norm
            b[at(i), at(j)] = value
            put(value, i, j, bh, bl)

    step = 2 * BLK

    def product(p, lh, ll, rh, rl):
        take, rest = slice(p * step, (p + 1) * step), slice(p * step, width)
        return (
            jnp.dot(lh[take, :], rh[:, rest], preferred_element_type=F32)
            + jnp.dot(lh[take, :], rl[:, rest], preferred_element_type=F32)
            + jnp.dot(ll[take, :], rh[:, rest], preferred_element_type=F32)
        )

    for p in range(NB // 2):
        b2[p * step:(p + 1) * step, p * step:] = product(p, bh, bl, bh, bl)
    for i in range(NB):
        for j in range(i, NB):
            value = b2[at(i), at(j)]
            put(value, i, j, ph, pp)
            put(value - 9.0 * b[at(i), at(j)], i, j, qh, ql)
    scale = lax.rsqrt(norm) / 16.0
    for p in range(NB // 2):
        high_part = product(p, ph, pp, qh, ql)
        for i in (2 * p, 2 * p + 1):
            for j in range(i, NB):
                value = high_part[(i - 2 * p) * BLK:(i - 2 * p + 1) * BLK, (j - 2 * p) * BLK:(j - 2 * p + 1) * BLK]
                value = value + (27.0 * b2[at(i), at(j)] - 39.0 * b[at(i), at(j)])
                if i == j:
                    value = value + 36.0 * eye
                put(value * scale, i, j, bh, bl)

    line = jnp.concatenate([center[i:i + 1, :] for i in range(NB)], axis=1)
    c_high, c_rest = split(line)
    c_rest = line - c_high.astype(F32)
    c_mid = c_rest.astype(BF16).astype(F32)
    c_low = c_rest - c_mid
    which = lax.broadcasted_iota(jnp.int32, (16, width), 0)
    parts = jnp.where(
        which == 0, c_high.astype(F32),
        jnp.where(which == 1, c_mid, jnp.where(which == 2, c_low, 0.0)),
    ).astype(BF16)
    shift = jnp.dot(parts, bh[...], preferred_element_type=F32) + jnp.dot(
        parts, bl[...], preferred_element_type=F32
    )
    shift = jnp.sum(shift, axis=0, keepdims=True)
    for r in range(0, x_ref.shape[0], step):
        for c in range(0, width, 2 * step):
            value = jnp.dot(x_ref[r:r + step, :], bh[:, c:c + 2 * step], preferred_element_type=F32)
            value += jnp.dot(x_ref[r:r + step, :], bl[:, c:c + 2 * step], preferred_element_type=F32)
            o_ref[r:r + step, c:c + 2 * step] = (value - shift[:, c:c + 2 * step]).astype(BF16)


def white(pooled, x):
    width = NB * BLK
    whole = pl.BlockSpec(memory_space=pltpu.VMEM)
    return pl.pallas_call(
        white_kernel,
        name="white",
        out_shape=jax.ShapeDtypeStruct(x.shape, BF16),
        in_specs=[whole, whole],
        out_specs=whole,
        scratch_shapes=[pltpu.VMEM((width, width), F32)] * 2 + [pltpu.VMEM((width, width), BF16)] * 6,
        compiler_params=pltpu.CompilerParams(vmem_limit_bytes=48 * 2**20),
    )(pooled, x)


def on_device(embeddings, valid):
    return white(pool(embeddings, valid[None, :]), embeddings)


def solution(mesh):
    in_specs = (P(("wide", "narrow"), None), P(("wide", "narrow")))
    return jax.shard_map(
        on_device, mesh=mesh, in_specs=in_specs, out_specs=P(("wide", "narrow"), None), check_vma=False
    )
```

time: 494 us -> 78.9 us (0.16)
  blocking collectives: 163 us -> 0 us
  waiting for transfers between devices: 158 us -> 0 us
  Pallas kernels: 0 us -> 76.8 us
  other arithmetic: 60.5 us -> 0 us
  loops' own time: 42.7 us -> 0 us
  matrix products: 27.4 us -> 0 us
  local copies, waits for them, and re-layouts: 23.1 us -> 1.91 us
  between operations: 15.4 us -> 0.02 us
    all_gather x3 -> x0, waiting for transfers between devices: 95.2 us -> none  [the longest x1 43.9 us: on_device(): lax.all_gather(root_rows, 'narrow', axis=0, tiled=True)]
    pallas_call x0 -> x2, Pallas kernels: none -> 76.8 us  [the longest x1 62.2 us: pool(): pl.pallas_call(pool_kernel, name='pool', out_shape=jax.ShapeDtypeStruct((...]
    psum x2 -> x0, blocking collectives: 68.6 us -> none  [the longest x1 37.7 us: on_device(): trace_cov, square_sum = lax.psum((trace_part, square_part), 'narrow')]
    reduce_scatter x1 -> x0, waiting for transfers between devices: 62.6 us -> none  [narrow_rows(): return lax.psum_scatter(term, 'narrow', scatter_dimension=0, tiled=True)]
    unnamed x1 -> x0, blocking collectives: 59.3 us -> none
    another operation x1 -> x0, loops' own time: 42.7 us -> none  [merged(): lax.fori_loop(1, lax.axis_size(axis), lambda source, state: combine(state...]
    all_gather x1 -> x0, blocking collectives: 35 us -> none  [merged(): gathered = jax.tree.map(lambda a: lax.all_gather(a, axis), part)]
    add x32 -> x0, other arithmetic: 32.3 us -> none  [the longest x31 32.3 us: pooled(): return (joined, left_sums + right_sums, left_rows + right_rows + extra)]
  transfers between devices with their start and end apart: 4 -> 0, of which waited for: 4 -> 0; matrix products, arithmetic and copies ran while one was open for 1% -> 0% of each run, Pallas kernels for 0% -> 0%
where the time goes in v1:
time: 78.9 us; the launch traced here: 78.7 us
  Pallas kernels  76.8 us (97%)
  local copies, waits for them, and re-layouts  1.91 us (2%)
    pallas_call x1, Pallas kernels, pool(): pl.pallas_call(pool_kernel, name='pool', out_shape=jax.ShapeDtypeStruct((...  62.2 us
    pallas_call x1, Pallas kernels, white(): pl.pallas_call(white_kernel, name='white', out_shape=jax.ShapeDtypeStruct...  14.6 us
    unnamed x6, local copies, waits for them, and re-layouts  1.91 us

profile of v1, /device:TPU:1, one launch (start us, length us, event | category | flops | bytes accessed | tf_op | source)
XLA Modules:
  0.0 78.7 jit_solution(6163045525979186524)
XLA Ops:
  0.0 0.0 copy-start
  0.0 1.2 %copy-done = bf16[512,1024]{1,0:T(8,128)(2,1)S(1)} copy-done((bf16[512,1024]{1,0:T(8,128)(2,1)S(1)}, bf16[512,1024]{1,0:T(8,128)(2,1)}, u32[]{:S(2)}) %copy-start) | copy-done | bytes 1048600
  1.2 0.0 copy-start.2
  1.2 0.7 copy-done.2
  1.9 0.0 copy-start.1
  1.9 62.2 %pool.1.f_ref = f32[2,2312,128]{2,1,0:T(8,128)S(1)} custom-call(bf16[512,1024]{1,0:T(8,128)(2,1)S(1)} %copy-done, s32[1,512]{1,0:T(1,128)S(1)} %bitcast.1), custom_call_target="tpu_custom_call" | custom-call | tf_op jit(solution)/shard_map/pool/pallas_call | solution.py:217
  64.1 0.0 copy-done.1
  64.1 14.6 %white.1 = bf16[512,1024]{1,0:T(8,128)(2,1)} custom-call(f32[2,2312,128]{2,1,0:T(8,128)S(1)} %pool.1.f_ref, bf16[512,1024]{1,0:T(8,128)(2,1)S(1)} %copy-done.1), custom_call_target="tpu_custom_call" | custom-call | tf_op jit(solution)/shard_map/white/pallas_call | solution.py:347
Async XLA Ops:
  0.0 1.2 %copy-start = (bf16[512,1024]{1,0:T(8,128)(2,1)S(1)}, bf16[512,1024]{1,0:T(8,128)(2,1)}, u32[]{:S(2)}) copy-start(bf16[512,1024]{1,0:T(8,128)(2,1)} %x_ref.3) | copy-start | bytes 3145732
  1.2 0.7 copy-start.2
  1.9 62.2 %copy-start.1 = (bf16[512,1024]{1,0:T(8,128)(2,1)S(1)}, bf16[512,1024]{1,0:T(8,128)(2,1)}, u32[]{:S(2)}) copy-start(bf16[512,1024]{1,0:T(8,128)(2,1)} %x_ref.3) | copy-start | bytes 3145732

commit v2 on v1

v2 whole, which is shorter than its diff:
```python
import functools

import jax
import jax.numpy as jnp
from jax import lax
from jax.experimental import pallas as pl
from jax.experimental.pallas import tpu as pltpu
from jax.sharding import PartitionSpec as P

MESH = pl.DeviceIdType.MESH
F32 = jnp.float32
BF16 = jnp.bfloat16

SIZE = {"z": 8, "x": 4, "y": 8, "c": 2}
BLK = 128
NB = 8
HALF_ROWS = ((0, 3, 4, 7), (1, 2, 5, 6))
A1X, A2X = 192, 128
AX = A1X + A2X
A1P, A2P = A1X // 8, A2X // 8
BY, BX = 64, 16
B0 = 4 * AX
C0 = B0 + 8 * BY
D0 = C0 + 8 * BY
HALF = D0 + 8
GX = AX + 8
GB = 4 * GX
GC = GB + 8 * BY
GHALF = GC + 8 * BY
N_COPIES = 120
FAR_8 = (4, 3, 5, 2, 6, 1, 7)
FAR_4 = (2, 1, 3)


def block_place(i, j):
    half = 0 if i in HALF_ROWS[0] else 1
    row = 0
    for k in HALF_ROWS[half]:
        if k == i:
            break
        row += NB - k
    return half, (row + j - i) * BLK


def coords():
    w, n = lax.axis_index("wide"), lax.axis_index("narrow")
    return {"z": w // 4, "x": w % 4, "y": n // 2, "c": n % 2}


def moved(me, axis, step):
    at = dict(me)
    at[axis] = lax.rem(me[axis] + step + SIZE[axis], SIZE[axis])
    return at


def ident(at):
    return (at["z"] * 4 + at["x"], at["y"] * 2 + at["c"])


def order(axis):
    return {"x": FAR_4, "y": FAR_8, "z": FAR_8, "c": (1,)}[axis]


def rows(start, size):
    return pl.ds(pl.multiple_of(start, 8), size)


def summed_row(row):
    return row // AX * GX + row % AX if row < B0 else row - B0 + GB


def total(own, parts):
    value = own
    for k in range(parts.shape[0]):
        value = value + parts[k]
    return value


def pool_kernel(
    x_hbm, valid_hbm, out_ref,
    x_ref, valid_ref, g, got, acc,
    r1x, r1y, r1z, s1a, s1e, s1x, r2x, r2y, r2z, s2z, s2y, r3z, r3y,
    load_sem, send_sem, recv_sem,
):
    me = coords()
    core = me["c"]
    barrier = pltpu.get_barrier_semaphore()
    count = 0
    for axis in ("z", "y", "x", "c"):
        for step in order(axis):
            pl.semaphore_signal(
                barrier, inc=1, device_id=ident(moved(me, axis, step)), device_id_type=MESH
            )
            count += 1
    loads = [
        pltpu.make_async_copy(x_hbm, x_ref, load_sem.at[0]),
        pltpu.make_async_copy(valid_hbm, valid_ref, load_sem.at[1]),
    ]
    for load in loads:
        load.start()
    for load in loads:
        load.wait()

    mask = valid_ref[...].astype(F32)
    mask_half = mask.astype(BF16)
    for half in range(2):
        for i in HALF_ROWS[half]:
            left = x_ref[:, i * BLK:(i + 1) * BLK].T * mask_half
            panel = jnp.dot(left, x_ref[:, i * BLK:], preferred_element_type=F32)
            for j in range(i, NB):
                _, row = block_place(i, j)
                for k in range(0, BLK, 64):
                    to = summed_row(row + k)
                    g[half, to:to + 64, :] = panel[k:k + 64, (j - i) * BLK:(j - i + 1) * BLK]
    sums = jnp.dot(
        jnp.broadcast_to(mask_half, (16, mask.shape[1])), x_ref[...], preferred_element_type=F32
    )
    valid_count = jnp.broadcast_to(jnp.sum(mask, axis=1, keepdims=True), (8, BLK))
    for part in range(4):
        to = part * GX + AX
        for i in range(NB):
            g[0, to + i:to + i + 1, :] = sums[0:1, i * BLK:(i + 1) * BLK]
        g[1, to:to + 8, :] = valid_count

    pl.semaphore_wait(barrier, count)

    used = []

    def copy(src, dst, axis, step):
        at = len(used)
        made = pltpu.make_async_remote_copy(
            src_ref=src, dst_ref=dst, send_sem=send_sem.at[at], recv_sem=recv_sem.at[at],
            device_id=ident(moved(me, axis, step)), device_id_type=MESH,
        )
        used.append(made)
        made.start()
        return made

    def arrive(copies):
        for made in copies:
            made.wait_recv()

    def beside(axis, step):
        return moved(me, axis, step)[axis]

    cuts = [pl.ds(GB, GHALF - GB)] + [rows(GX * beside("x", s), GX) for s in FAR_4 + (0,)]
    pair = [copy(g.at[1 - core, cut], got.at[cut], "c", 1) for cut in cuts]

    def add_pair(k):
        pair[k].wait_recv()
        acc[cuts[k], :] = g[core, cuts[k], :] + got[cuts[k], :]

    add_pair(0)
    w1y, w1z = [], []
    for s in FAR_8:
        w1y.append(copy(acc.at[rows(GB + BY * beside("y", s), BY)], r1y.at[s - 1], "y", s))
        w1z.append(copy(acc.at[rows(GC + BY * beside("z", s), BY)], r1z.at[s - 1], "z", s))
    w1x = []
    for k, s in enumerate(FAR_4):
        add_pair(k + 1)
        w1x.append(copy(acc.at[cuts[k + 1]], r1x.at[s - 1], "x", s))
    add_pair(4)

    arrive(w1x)
    s1a[...] = total(acc[rows(GX * me["x"], GX), :], r1x)
    w2y = [copy(s1a.at[rows(A1P * beside("y", s), A1P)], r2y.at[s - 1], "y", s) for s in FAR_8]
    for k in range(8):
        s1e[k, 0:A2P, :] = s1a[A1X + A2P * k:A1X + A2P * (k + 1), :]
        s1e[k, A2P:A2P + 8, :] = s1a[AX:GX, :]
    w2z = [copy(s1e.at[beside("z", s)], r2z.at[s - 1], "z", s) for s in FAR_8]
    arrive(w1y)
    value = total(acc[rows(GB + BY * me["y"], BY), :], r1y)
    for k in range(4):
        s1x[k, 0:BX, :] = value[BX * k:BX * (k + 1), :]
    arrive(w1z)
    value = total(acc[rows(GC + BY * me["z"], BY), :], r1z)
    for k in range(4):
        s1x[k, BX:2 * BX, :] = value[BX * k:BX * (k + 1), :]
    w2x = [copy(s1x.at[beside("x", s)], r2x.at[s - 1], "x", s) for s in FAR_4]

    arrive(w2y)
    s2z[0:A1P, :] = total(s1a[rows(A1P * me["y"], A1P), :], r2y)
    arrive(w2x)
    value = total(s1x[me["x"]], r2x)
    s2z[A1P:A1P + BX, :] = value[0:BX, :]
    w3z = [copy(s2z, r3z.at[s - 1], "z", s) for s in FAR_8]
    s2y[A2P + 8:A2P + 8 + BX, :] = value[BX:2 * BX, :]
    arrive(w2z)
    s2y[0:A2P + 8, :] = total(s1e[me["z"]], r2z)
    w3y = [copy(s2y, r3y.at[s - 1], "y", s) for s in FAR_8]

    def share(start, size, axis):
        piece = out_ref.at[core, rows(start, size)]
        return [copy(piece, piece, axis, s) for s in order(axis)]

    ax = AX * me["x"]
    a_at, e_at = ax + A1P * me["y"], ax + A1X + A2P * me["z"]
    b_at, c_at = B0 + BY * me["y"], C0 + BY * me["z"]
    arrive(w3z)
    value = total(s2z[...], r3z)
    out_ref[core, rows(b_at + BX * me["x"], BX), :] = value[A1P:A1P + BX, :]
    w4b = share(b_at + BX * me["x"], BX, "x")
    out_ref[core, rows(a_at, A1P), :] = value[0:A1P, :]
    w4a = share(a_at, A1P, "y")
    arrive(w3y)
    value = total(s2y[...], r3y)
    out_ref[core, rows(c_at + BX * me["x"], BX), :] = value[A2P + 8:A2P + 8 + BX, :]
    w4c = share(c_at + BX * me["x"], BX, "x")
    out_ref[core, rows(e_at, A2P), :] = value[0:A2P, :]
    w4e = share(e_at, A2P, "z")
    out_ref[core, D0:HALF, :] = value[A2P:A2P + 8, :]

    arrive(w4b)
    w5b = share(b_at, BY, "y")
    arrive(w4c)
    w5c = share(c_at, BY, "z")
    arrive(w4a)
    w5a = share(ax, A1X, "x")
    arrive(w4e)
    w5e = share(ax + A1X, A2X, "x")
    w6 = share(D0, 8, "c") + share(ax, AX, "c") + share(b_at, BY, "c") + share(c_at, BY, "c")
    for s in (1, 7, 2, 6, 3, 5, 4):
        k = FAR_8.index(s)
        w5b[k].wait_recv()
        w6 += share(B0 + BY * beside("y", -s), BY, "c")
        w5c[k].wait_recv()
        w6 += share(C0 + BY * beside("z", -s), BY, "c")
        if s in (7, 6, 5):
            k = (7, 6, 5).index(s)
            s = (1, 3, 2)[k]
            k = FAR_4.index(s)
            w5a[k].wait_recv()
            w5e[k].wait_recv()
            w6 += share(AX * beside("x", -s), AX, "c")
    arrive(w6)
    for made in used:
        made.wait_send()


def pool(x, valid):
    part = lambda n, r: pltpu.VMEM((n, r, BLK), F32)
    flat = lambda r: pltpu.VMEM((r, BLK), F32)
    return pl.pallas_call(
        pool_kernel,
        name="pool",
        out_shape=jax.ShapeDtypeStruct((2, HALF, BLK), F32),
        in_specs=[pl.BlockSpec(memory_space=pltpu.HBM)] * 2,
        out_specs=pl.BlockSpec(memory_space=pltpu.VMEM),
        scratch_shapes=[
            pltpu.VMEM(x.shape, BF16), pltpu.VMEM(valid.shape, jnp.int32),
            part(2, GHALF), flat(GHALF), flat(GHALF),
            part(3, GX), part(7, BY), part(7, BY),
            flat(GX), part(8, A2P + 8), part(4, 2 * BX),
            part(3, 2 * BX), part(7, A1P), part(7, A2P + 8),
            flat(A1P + BX), flat(A2P + 8 + BX), part(7, A1P + BX), part(7, A2P + 8 + BX),
            pltpu.SemaphoreType.DMA((2,)),
            pltpu.SemaphoreType.DMA((N_COPIES,)), pltpu.SemaphoreType.DMA((N_COPIES,)),
        ],
        compiler_params=pltpu.CompilerParams(
            collective_id=0, has_side_effects=True, vmem_limit_bytes=40 * 2**20
        ),
    )(x, valid)


def split(value):
    high = value.astype(BF16)
    return high, (value - high.astype(F32)).astype(BF16)


def white_kernel(f_ref, x_hbm, o_hbm, x_ref, o_ref, b, b2, bh, bl, sh, sl, load_sem, store_sem):
    width = NB * BLK
    n_rows = x_hbm.shape[0]
    load = pltpu.make_async_copy(x_hbm, x_ref.at[pl.ds(0, n_rows)], load_sem)
    load.start()
    count = f_ref[1, D0:D0 + 1, :]
    inverse = 1.0 / count
    sums = f_ref[0, D0:D0 + 8, :]
    center = sums / count
    diag = (
        lax.broadcasted_iota(jnp.int32, (BLK, BLK), 0)
        == lax.broadcasted_iota(jnp.int32, (BLK, BLK), 1)
    )
    eye = diag.astype(F32)

    def at(i):
        return slice(i * BLK, (i + 1) * BLK)

    trace = jnp.zeros((BLK, BLK), F32)
    square = jnp.zeros((BLK, BLK), F32)
    for i in range(NB):
        column = jnp.broadcast_to(sums[i:i + 1, :], (BLK, BLK)).T
        for j in range(i, NB):
            half, row = block_place(i, j)
            scatter = f_ref[half, row:row + BLK, :] - column * center[j:j + 1, :]
            cov = scatter * inverse
            if i == j:
                trace = trace + jnp.where(diag, cov, 0.0)
                square = square + cov * cov
            else:
                square = square + 2.0 * (cov * cov)
            b[at(i), at(j)] = cov
    trace = jnp.sum(trace, axis=(0, 1), keepdims=True)
    square = jnp.sum(square, axis=(0, 1), keepdims=True)
    ridge = 0.05 * trace / width + 1e-06
    norm = jnp.sqrt(square + 2.0 * ridge * trace + width * ridge * ridge)
    inv_norm = 1.0 / norm

    def put(value, i, j, high, low):
        h, l = split(value)
        high[at(i), at(j)] = h
        low[at(i), at(j)] = l
        if i != j:
            h, l = split(value.T)
            high[at(j), at(i)] = h
            low[at(j), at(i)] = l

    for i in range(NB):
        for j in range(i, NB):
            value = b[at(i), at(j)]
            if i == j:
                value = value + ridge * eye
            value = value * inv_norm
            b[at(i), at(j)] = value
            put(value, i, j, bh, bl)

    step = 2 * BLK

    def square_of(p, high, low):
        take, rest = slice(p * step, (p + 1) * step), slice(p * step, width)
        return (
            jnp.dot(high[take, :], high[:, rest], preferred_element_type=F32)
            + jnp.dot(high[take, :], low[:, rest], preferred_element_type=F32)
            + jnp.dot(low[take, :], high[:, rest], preferred_element_type=F32)
        )

    def blocks(p, panel):
        for i in (2 * p, 2 * p + 1):
            for j in range(i, NB):
                r, c = i - 2 * p, j - 2 * p
                yield i, j, panel[r * BLK:(r + 1) * BLK, c * BLK:(c + 1) * BLK]

    for p in range(NB // 2):
        for i, j, value in blocks(p, square_of(p, bh, bl)):
            own = b[at(i), at(j)]
            put(value - 4.5 * own, i, j, sh, sl)
            value = 6.75 * value - 39.0 * own
            b2[at(i), at(j)] = value + 36.0 * eye if i == j else value
    scale = lax.rsqrt(norm) / 16.0
    for p in range(NB // 2):
        for i, j, value in blocks(p, square_of(p, sh, sl)):
            put((value + b2[at(i), at(j)]) * scale, i, j, bh, bl)

    line = jnp.concatenate([center[i:i + 1, :] for i in range(NB)], axis=1)
    c_high = line.astype(BF16).astype(F32)
    c_mid = (line - c_high).astype(BF16).astype(F32)
    c_low = line - c_high - c_mid
    which = lax.broadcasted_iota(jnp.int32, (16, width), 0)
    x_ref[n_rows:n_rows + 16, :] = jnp.where(
        which == 0, c_high,
        jnp.where(which == 1, c_mid, jnp.where(which == 2, c_low, 0.0)),
    ).astype(BF16)
    load.wait()
    stores = []
    for k in range(width // step):
        cols = slice(k * step, (k + 1) * step)
        value = jnp.dot(x_ref[...], bh[:, cols], preferred_element_type=F32) + jnp.dot(
            x_ref[...], bl[:, cols], preferred_element_type=F32
        )
        shift = jnp.sum(value[n_rows:, :], axis=0, keepdims=True)
        o_ref[:, cols] = (value[:n_rows, :] - shift).astype(BF16)
        cols = pl.ds(k * step, step)
        store = pltpu.make_async_copy(o_ref.at[:, cols], o_hbm.at[:, cols], store_sem.at[k])
        store.start()
        stores.append(store)
    for store in stores:
        store.wait()


def white(pooled, x):
    width = NB * BLK
    hbm = pl.BlockSpec(memory_space=pltpu.HBM)
    return pl.pallas_call(
        white_kernel,
        name="white",
        out_shape=jax.ShapeDtypeStruct(x.shape, BF16),
        in_specs=[pl.BlockSpec(memory_space=pltpu.VMEM), hbm],
        out_specs=hbm,
        scratch_shapes=[pltpu.VMEM((x.shape[0] + 16, width), BF16), pltpu.VMEM(x.shape, BF16)]
        + [pltpu.VMEM((width, width), F32)] * 2
        + [pltpu.VMEM((width, width), BF16)] * 4
        + [pltpu.SemaphoreType.DMA, pltpu.SemaphoreType.DMA((width // (2 * BLK),))],
        compiler_params=pltpu.CompilerParams(vmem_limit_bytes=48 * 2**20),
    )(pooled, x)


def on_device(embeddings, valid):
    return white(pool(embeddings, valid[None, :]), embeddings)


def solution(mesh):
    in_specs = (P(("wide", "narrow"), None), P(("wide", "narrow")))
    return jax.shard_map(
        on_device, mesh=mesh, in_specs=in_specs, out_specs=P(("wide", "narrow"), None), check_vma=False
    )
```

time: 78.9 us -> 71.8 us (0.910)
  Pallas kernels: 76.8 us -> 69.6 us
    pallas_call x1, Pallas kernels: 62.2 us -> 55.6 us  [pool(): pl.pallas_call(pool_kernel, name='pool', out_shape=jax.ShapeDtypeStruct((...]
where the time goes in v2:
time: 71.8 us; the launch traced here: 71.7 us
  Pallas kernels  69.6 us (97%)
  local copies, waits for them, and re-layouts  1.91 us (3%)
    pallas_call x1, Pallas kernels, pool(): pl.pallas_call(pool_kernel, name='pool', out_shape=jax.ShapeDtypeStruct((...  55.6 us
    pallas_call x1, Pallas kernels, white(): pl.pallas_call(white_kernel, name='white', out_shape=jax.ShapeDtypeStruct...  14 us
    unnamed x6, local copies, waits for them, and re-layouts  1.91 us

profile of v2, /device:TPU:1, one launch (start us, length us, event | category | flops | bytes accessed | tf_op | source)
XLA Modules:
  0.0 71.7 jit_solution(1499632437185156153)
XLA Ops:
  0.0 0.0 copy-start
  0.0 1.2 %copy-done = bf16[512,1024]{1,0:T(8,128)(2,1)S(1)} copy-done((bf16[512,1024]{1,0:T(8,128)(2,1)S(1)}, bf16[512,1024]{1,0:T(8,128)(2,1)}, u32[]{:S(2)}) %copy-start) | copy-done | bytes 1048600
  1.2 0.0 copy-start.2
  1.2 0.7 copy-done.2
  1.9 0.0 copy-start.1
  1.9 55.6 %pool.1.f_ref = f32[2,2312,128]{2,1,0:T(8,128)S(1)} custom-call(bf16[512,1024]{1,0:T(8,128)(2,1)S(1)} %copy-done, s32[1,512]{1,0:T(1,128)S(1)} %bitcast.1), custom_call_target="tpu_custom_call" | custom-call | tf_op jit(solution)/shard_map/pool/pallas_call | solution.py:243
  57.5 0.0 copy-done.1
  57.5 14.0 %white.1 = bf16[512,1024]{1,0:T(8,128)(2,1)} custom-call(f32[2,2312,128]{2,1,0:T(8,128)S(1)} %pool.1.f_ref, bf16[512,1024]{1,0:T(8,128)(2,1)S(1)} %copy-done.1), custom_call_target="tpu_custom_call" | custom-call | tf_op jit(solution)/shard_map/white/pallas_call | solution.py:382
Async XLA Ops:
  0.0 1.2 %copy-start = (bf16[512,1024]{1,0:T(8,128)(2,1)S(1)}, bf16[512,1024]{1,0:T(8,128)(2,1)}, u32[]{:S(2)}) copy-start(bf16[512,1024]{1,0:T(8,128)(2,1)} %x_hbm.3) | copy-start | bytes 3145732
  1.2 0.7 copy-start.2
  1.9 55.6 %copy-start.1 = (bf16[512,1024]{1,0:T(8,128)(2,1)S(1)}, bf16[512,1024]{1,0:T(8,128)(2,1)}, u32[]{:S(2)}) copy-start(bf16[512,1024]{1,0:T(8,128)(2,1)} %x_hbm.3) | copy-start | bytes 3145732

commit v3 on v2

--- a/solution.py
+++ b/solution.py
@@ -267,7 +267,7 @@
     return high, (value - high.astype(F32)).astype(BF16)
 
 
-def white_kernel(f_ref, x_hbm, o_hbm, x_ref, o_ref, b, b2, bh, bl, sh, sl, load_sem, store_sem):
+def white_kernel(f_ref, x_hbm, o_hbm, x_ref, o_ref, b, hh, hl, bh, bl, sh, sl, load_sem, store_sem):
     width = NB * BLK
     n_rows = x_hbm.shape[0]
     load = pltpu.make_async_copy(x_hbm, x_ref.at[pl.ds(0, n_rows)], load_sem)
@@ -284,6 +284,15 @@
 
     def at(i):
         return slice(i * BLK, (i + 1) * BLK)
+
+    def put(value, i, j, high, low):
+        h, l = split(value)
+        high[at(i), at(j)] = h
+        low[at(i), at(j)] = l
+        if i != j:
+            h, l = split(value.T)
+            high[at(j), at(i)] = h
+            low[at(j), at(i)] = l
 
     trace = jnp.zeros((BLK, BLK), F32)
     square = jnp.zeros((BLK, BLK), F32)
@@ -299,56 +308,43 @@
             else:
                 square = square + 2.0 * (cov * cov)
             b[at(i), at(j)] = cov
+            put(cov, i, j, bh, bl)
+
+    step = 2 * BLK
+
+    def squared(high, low, use):
+        for p in range(NB // 2):
+            take, rest = slice(p * step, (p + 1) * step), slice(p * step, width)
+            hh[take, rest] = jnp.dot(high[take, :], high[:, rest], preferred_element_type=F32)
+            hl[take, :] = jnp.dot(high[take, :], low[...], preferred_element_type=F32)
+            for j in (2 * p, 2 * p + 1):
+                for i in range(j + 1):
+                    use(i, j, hh[at(i), at(j)] + (hl[at(i), at(j)] + hl[at(j), at(i)].T))
+
     trace = jnp.sum(trace, axis=(0, 1), keepdims=True)
     square = jnp.sum(square, axis=(0, 1), keepdims=True)
     ridge = 0.05 * trace / width + 1e-06
     norm = jnp.sqrt(square + 2.0 * ridge * trace + width * ridge * ridge)
     inv_norm = 1.0 / norm
-
-    def put(value, i, j, high, low):
-        h, l = split(value)
-        high[at(i), at(j)] = h
-        low[at(i), at(j)] = l
-        if i != j:
-            h, l = split(value.T)
-            high[at(j), at(i)] = h
-            low[at(j), at(i)] = l
-
-    for i in range(NB):
-        for j in range(i, NB):
-            value = b[at(i), at(j)]
-            if i == j:
-                value = value + ridge * eye
-            value = value * inv_norm
-            b[at(i), at(j)] = value
-            put(value, i, j, bh, bl)
-
-    step = 2 * BLK
-
-    def square_of(p, high, low):
-        take, rest = slice(p * step, (p + 1) * step), slice(p * step, width)
-        return (
-            jnp.dot(high[take, :], high[:, rest], preferred_element_type=F32)
-            + jnp.dot(high[take, :], low[:, rest], preferred_element_type=F32)
-            + jnp.dot(low[take, :], high[:, rest], preferred_element_type=F32)
-        )
-
-    def blocks(p, panel):
-        for i in (2 * p, 2 * p + 1):
-            for j in range(i, NB):
-                r, c = i - 2 * p, j - 2 * p
-                yield i, j, panel[r * BLK:(r + 1) * BLK, c * BLK:(c + 1) * BLK]
-
-    for p in range(NB // 2):
-        for i, j, value in blocks(p, square_of(p, bh, bl)):
-            own = b[at(i), at(j)]
-            put(value - 4.5 * own, i, j, sh, sl)
-            value = 6.75 * value - 39.0 * own
-            b2[at(i), at(j)] = value + 36.0 * eye if i == j else value
+    inv_norm2 = inv_norm * inv_norm
     scale = lax.rsqrt(norm) / 16.0
-    for p in range(NB // 2):
-        for i, j, value in blocks(p, square_of(p, sh, sl)):
-            put((value + b2[at(i), at(j)]) * scale, i, j, bh, bl)
+
+    def half_way(i, j, value):
+        cov = b[at(i), at(j)]
+        value = value + (2.0 * ridge) * cov
+        if i == j:
+            value = value + (ridge * ridge) * eye
+            cov = cov + ridge * eye
+        base, base2 = cov * inv_norm, value * inv_norm2
+        put(base2 - 4.5 * base, i, j, sh, sl)
+        rest = 6.75 * base2 - 39.0 * base
+        b[at(i), at(j)] = rest + 36.0 * eye if i == j else rest
+
+    def rooted(i, j, value):
+        put((value + b[at(i), at(j)]) * scale, i, j, bh, bl)
+
+    squared(bh, bl, half_way)
+    squared(sh, sl, rooted)
 
     line = jnp.concatenate([center[i:i + 1, :] for i in range(NB)], axis=1)
     c_high = line.astype(BF16).astype(F32)
@@ -386,7 +382,7 @@
         in_specs=[pl.BlockSpec(memory_space=pltpu.VMEM), hbm],
         out_specs=hbm,
         scratch_shapes=[pltpu.VMEM((x.shape[0] + 16, width), BF16), pltpu.VMEM(x.shape, BF16)]
-        + [pltpu.VMEM((width, width), F32)] * 2
+        + [pltpu.VMEM((width, width), F32)] * 3
         + [pltpu.VMEM((width, width), BF16)] * 4
         + [pltpu.SemaphoreType.DMA, pltpu.SemaphoreType.DMA((width // (2 * BLK),))],
         compiler_params=pltpu.CompilerParams(vmem_limit_bytes=48 * 2**20),
@@ -394,7 +390,9 @@
 
 
 def on_device(embeddings, valid):
-    return white(pool(embeddings, valid[None, :]), embeddings)
+    embeddings = pltpu.with_memory_space_constraint(embeddings, pltpu.HBM)
+    valid = pltpu.with_memory_space_constraint(valid[None, :], pltpu.HBM)
+    return white(pool(embeddings, valid), embeddings)
 
 
 def solution(mesh):

time: 71.8 us -> 68.3 us (0.951)
  local copies, waits for them, and re-layouts: 1.91 us -> 0 us
  Pallas kernels: 69.6 us -> 68.1 us
    unnamed x6 -> x0, local copies, waits for them, and re-layouts: 1.91 us -> none
    pallas_call x1, Pallas kernels: 14 us -> 12.7 us  [white(): pl.pallas_call(white_kernel, name='white', out_shape=jax.ShapeDtypeStruct...]
where the time goes in v3:
time: 68.3 us; the launch traced here: 68.1 us
  Pallas kernels  68.1 us (100%)
    pallas_call x1, Pallas kernels, pool(): pl.pallas_call(pool_kernel, name='pool', out_shape=jax.ShapeDtypeStruct((...  55.5 us
    pallas_call x1, Pallas kernels, white(): pl.pallas_call(white_kernel, name='white', out_shape=jax.ShapeDtypeStruct...  12.7 us

profile of v3, /device:TPU:1, one launch (start us, length us, event | category | flops | bytes accessed | tf_op | source)
XLA Modules:
  0.0 68.1 jit_solution(9761431829250501645)
XLA Ops:
  0.0 55.5 %pool.1.f_ref = f32[2,2312,128]{2,1,0:T(8,128)S(1)} custom-call(bf16[512,1024]{1,0:T(8,128)(2,1)} %x_hbm.3, s32[1,512]{1,0:T(1,128)} %bitcast.1), custom_call_target="tpu_custom_call" | custom-call | tf_op jit(solution)/shard_map/pool/pallas_call | solution.py:243
  55.5 12.7 %white.1 = bf16[512,1024]{1,0:T(8,128)(2,1)} custom-call(f32[2,2312,128]{2,1,0:T(8,128)S(1)} %pool.1.f_ref, bf16[512,1024]{1,0:T(8,128)(2,1)} %x_hbm.3), custom_call_target="tpu_custom_call" | custom-call | tf_op jit(solution)/shard_map/white/pallas_call | solution.py:378

commit v4 on v3

--- a/solution.py
+++ b/solution.py
@@ -15,13 +15,14 @@
 BLK = 128
 NB = 8
 HALF_ROWS = ((0, 3, 4, 7), (1, 2, 5, 6))
-A1X, A2X = 192, 128
+A1X, A2X = 128, 128
 AX = A1X + A2X
 A1P, A2P = A1X // 8, A2X // 8
-BY, BX = 64, 16
+BY, BX = 80, 24
+BS = 4 * BX
 B0 = 4 * AX
-C0 = B0 + 8 * BY
-D0 = C0 + 8 * BY
+C0 = B0 + 8 * BS
+D0 = C0 + 8 * BS
 HALF = D0 + 8
 GX = AX + 8
 GB = 4 * GX
@@ -67,6 +68,24 @@
 
 def summed_row(row):
     return row // AX * GX + row % AX if row < B0 else row - B0 + GB
+
+
+def result_row(row):
+    if row < B0:
+        return row
+    place, row = divmod(row - B0, BY)
+    return B0 + place * BS + row
+
+
+def runs(row, where):
+    found = []
+    for k in range(0, BLK, 16):
+        to = where(row + k)
+        if found and found[-1][1] + found[-1][2] == to:
+            found[-1][2] += 16
+        else:
+            found.append([k, to, 16])
+    return found
 
 
 def total(own, parts):
@@ -86,12 +105,13 @@
     core = me["c"]
     barrier = pltpu.get_barrier_semaphore()
     count = 0
-    for axis in ("z", "y", "x", "c"):
-        for step in order(axis):
-            pl.semaphore_signal(
-                barrier, inc=1, device_id=ident(moved(me, axis, step)), device_id_type=MESH
-            )
-            count += 1
+    for axes in ("zy", "x", "c"):
+        for step in order(axes[0]):
+            for axis in axes:
+                pl.semaphore_signal(
+                    barrier, inc=1, device_id=ident(moved(me, axis, step)), device_id_type=MESH
+                )
+                count += 1
     loads = [
         pltpu.make_async_copy(x_hbm, x_ref, load_sem.at[0]),
         pltpu.make_async_copy(valid_hbm, valid_ref, load_sem.at[1]),
@@ -109,9 +129,8 @@
             panel = jnp.dot(left, x_ref[:, i * BLK:], preferred_element_type=F32)
             for j in range(i, NB):
                 _, row = block_place(i, j)
-                for k in range(0, BLK, 64):
-                    to = summed_row(row + k)
-                    g[half, to:to + 64, :] = panel[k:k + 64, (j - i) * BLK:(j - i + 1) * BLK]
+                for k, to, n in runs(row, summed_row):
+                    g[half, to:to + n, :] = panel[k:k + n, (j - i) * BLK:(j - i + 1) * BLK]
     sums = jnp.dot(
         jnp.broadcast_to(mask_half, (16, mask.shape[1])), x_ref[...], preferred_element_type=F32
     )
@@ -143,7 +162,8 @@
     def beside(axis, step):
         return moved(me, axis, step)[axis]
 
-    cuts = [pl.ds(GB, GHALF - GB)] + [rows(GX * beside("x", s), GX) for s in FAR_4 + (0,)]
+    cuts = [pl.ds(GB, 8 * BY), pl.ds(GC, 8 * BY)]
+    cuts += [rows(GX * beside("x", s), GX) for s in FAR_4 + (0,)]
     pair = [copy(g.at[1 - core, cut], got.at[cut], "c", 1) for cut in cuts]
 
     def add_pair(k):
@@ -151,15 +171,21 @@
         acc[cuts[k], :] = g[core, cuts[k], :] + got[cuts[k], :]
 
     add_pair(0)
-    w1y, w1z = [], []
-    for s in FAR_8:
-        w1y.append(copy(acc.at[rows(GB + BY * beside("y", s), BY)], r1y.at[s - 1], "y", s))
-        w1z.append(copy(acc.at[rows(GC + BY * beside("z", s), BY)], r1z.at[s - 1], "z", s))
+    w1y = [copy(acc.at[rows(GB + BY * beside("y", s), BY)], r1y.at[s - 1], "y", s) for s in FAR_8]
+    add_pair(1)
+    w1z = [copy(acc.at[rows(GC + BY * beside("z", s), BY)], r1z.at[s - 1], "z", s) for s in FAR_8]
     w1x = []
     for k, s in enumerate(FAR_4):
-        add_pair(k + 1)
-        w1x.append(copy(acc.at[cuts[k + 1]], r1x.at[s - 1], "x", s))
-    add_pair(4)
+        add_pair(k + 2)
+        w1x.append(copy(acc.at[cuts[k + 2]], r1x.at[s - 1], "x", s))
+    add_pair(5)
+
+    def quarters(value, first):
+        for k in range(4):
+            n = min(BX, BY - BX * k)
+            s1x[k, first:first + n, :] = value[BX * k:BX * k + n, :]
+            if n < BX:
+                s1x[k, first + n:first + BX, :] = jnp.zeros((BX - n, BLK), F32)
 
     arrive(w1x)
     s1a[...] = total(acc[rows(GX * me["x"], GX), :], r1x)
@@ -169,13 +195,9 @@
         s1e[k, A2P:A2P + 8, :] = s1a[AX:GX, :]
     w2z = [copy(s1e.at[beside("z", s)], r2z.at[s - 1], "z", s) for s in FAR_8]
     arrive(w1y)
-    value = total(acc[rows(GB + BY * me["y"], BY), :], r1y)
-    for k in range(4):
-        s1x[k, 0:BX, :] = value[BX * k:BX * (k + 1), :]
+    quarters(total(acc[rows(GB + BY * me["y"], BY), :], r1y), 0)
     arrive(w1z)
-    value = total(acc[rows(GC + BY * me["z"], BY), :], r1z)
-    for k in range(4):
-        s1x[k, BX:2 * BX, :] = value[BX * k:BX * (k + 1), :]
+    quarters(total(acc[rows(GC + BY * me["z"], BY), :], r1z), BX)
     w2x = [copy(s1x.at[beside("x", s)], r2x.at[s - 1], "x", s) for s in FAR_4]
 
     arrive(w2y)
@@ -195,7 +217,7 @@
 
     ax = AX * me["x"]
     a_at, e_at = ax + A1P * me["y"], ax + A1X + A2P * me["z"]
-    b_at, c_at = B0 + BY * me["y"], C0 + BY * me["z"]
+    b_at, c_at = B0 + BS * me["y"], C0 + BS * me["z"]
     arrive(w3z)
     value = total(s2z[...], r3z)
     out_ref[core, rows(b_at + BX * me["x"], BX), :] = value[A1P:A1P + BX, :]
@@ -222,9 +244,9 @@
     for s in (1, 7, 2, 6, 3, 5, 4):
         k = FAR_8.index(s)
         w5b[k].wait_recv()
-        w6 += share(B0 + BY * beside("y", -s), BY, "c")
+        w6 += share(B0 + BS * beside("y", -s), BY, "c")
         w5c[k].wait_recv()
-        w6 += share(C0 + BY * beside("z", -s), BY, "c")
+        w6 += share(C0 + BS * beside("z", -s), BY, "c")
         if s in (7, 6, 5):
             k = (7, 6, 5).index(s)
             s = (1, 3, 2)[k]
@@ -300,7 +322,10 @@
         column = jnp.broadcast_to(sums[i:i + 1, :], (BLK, BLK)).T
         for j in range(i, NB):
             half, row = block_place(i, j)
-            scatter = f_ref[half, row:row + BLK, :] - column * center[j:j + 1, :]
+            pooled = jnp.concatenate(
+                [f_ref[half, to:to + n, :] for _, to, n in runs(row, result_row)], axis=0
+            )
+            scatter = pooled - column * center[j:j + 1, :]
             cov = scatter * inverse
             if i == j:
                 trace = trace + jnp.where(diag, cov, 0.0)

time: 68.3 us -> 65.9 us (0.965)
  Pallas kernels: 68.1 us -> 65.8 us
    pallas_call x1, Pallas kernels: 55.5 us -> 53.1 us  [pool(): pl.pallas_call(pool_kernel, name='pool', out_shape=jax.ShapeDtypeStruct((...]
where the time goes in v4:
time: 65.9 us; the launch traced here: 65.8 us
  Pallas kernels  65.8 us (100%)
    pallas_call x1, Pallas kernels, pool(): pl.pallas_call(pool_kernel, name='pool', out_shape=jax.ShapeDtypeStruct((...  53.1 us
    pallas_call x1, Pallas kernels, white(): pl.pallas_call(white_kernel, name='white', out_shape=jax.ShapeDtypeStruct...  12.7 us

profile of v4, /device:TPU:1, one launch (start us, length us, event | category | flops | bytes accessed | tf_op | source)
XLA Modules:
  0.0 65.8 jit_solution(12649905633275826218)
XLA Ops:
  0.0 53.1 %pool.1.f_ref = f32[2,2568,128]{2,1,0:T(8,128)S(1)} custom-call(bf16[512,1024]{1,0:T(8,128)(2,1)} %x_hbm.3, s32[1,512]{1,0:T(1,128)} %bitcast.1), custom_call_target="tpu_custom_call" | custom-call | tf_op jit(solution)/shard_map/pool/pallas_call | solution.py:265
  53.1 12.7 %white.1 = bf16[512,1024]{1,0:T(8,128)(2,1)} custom-call(f32[2,2568,128]{2,1,0:T(8,128)S(1)} %pool.1.f_ref, bf16[512,1024]{1,0:T(8,128)(2,1)} %x_hbm.3), custom_call_target="tpu_custom_call" | custom-call | tf_op jit(solution)/shard_map/white/pallas_call | solution.py:403

commit v5 on v4

--- a/solution.py
+++ b/solution.py
@@ -155,6 +155,10 @@
         made.start()
         return made
 
+    def sent(copies):
+        for made in copies:
+            made.wait_send()
+
     def arrive(copies):
         for made in copies:
             made.wait_recv()
@@ -200,6 +204,7 @@
     quarters(total(acc[rows(GC + BY * me["z"], BY), :], r1z), BX)
     w2x = [copy(s1x.at[beside("x", s)], r2x.at[s - 1], "x", s) for s in FAR_4]
 
+    sent(pair)
     arrive(w2y)
     s2z[0:A1P, :] = total(s1a[rows(A1P * me["y"], A1P), :], r2y)
     arrive(w2x)
@@ -211,6 +216,7 @@
     s2y[0:A2P + 8, :] = total(s1e[me["z"]], r2z)
     w3y = [copy(s2y, r3y.at[s - 1], "y", s) for s in FAR_8]
 
+    sent(w1y + w1z + w1x)
     def share(start, size, axis):
         piece = out_ref.at[core, rows(start, size)]
         return [copy(piece, piece, axis, s) for s in order(axis)]
@@ -232,6 +238,7 @@
     w4e = share(e_at, A2P, "z")
     out_ref[core, D0:HALF, :] = value[A2P:A2P + 8, :]
 
+    sent(w2x + w2y + w2z)
     arrive(w4b)
     w5b = share(b_at, BY, "y")
     arrive(w4c)
@@ -241,6 +248,7 @@
     arrive(w4e)
     w5e = share(ax + A1X, A2X, "x")
     w6 = share(D0, 8, "c") + share(ax, AX, "c") + share(b_at, BY, "c") + share(c_at, BY, "c")
+    sent(w3z + w3y + w4b + w4c + w4a + w4e)
     for s in (1, 7, 2, 6, 3, 5, 4):
         k = FAR_8.index(s)
         w5b[k].wait_recv()
@@ -254,9 +262,9 @@
             w5a[k].wait_recv()
             w5e[k].wait_recv()
             w6 += share(AX * beside("x", -s), AX, "c")
+    sent(w5b + w5c + w5a + w5e)
     arrive(w6)
-    for made in used:
-        made.wait_send()
+    sent(w6)
 
 
 def pool(x, valid):
@@ -284,12 +292,15 @@
     )(x, valid)
 
 
+CHUNKS = ((0, 512), (512, 256), (768, 256))
+
+
 def split(value):
     high = value.astype(BF16)
     return high, (value - high.astype(F32)).astype(BF16)
 
 
-def white_kernel(f_ref, x_hbm, o_hbm, x_ref, o_ref, b, hh, hl, bh, bl, sh, sl, load_sem, store_sem):
+def white_kernel(f_ref, x_hbm, o_hbm, x_ref, o_ref, b, bh, bl, sh, sl, load_sem, store_sem):
     width = NB * BLK
     n_rows = x_hbm.shape[0]
     load = pltpu.make_async_copy(x_hbm, x_ref.at[pl.ds(0, n_rows)], load_sem)
@@ -340,11 +351,19 @@
     def squared(high, low, use):
         for p in range(NB // 2):
             take, rest = slice(p * step, (p + 1) * step), slice(p * step, width)
-            hh[take, rest] = jnp.dot(high[take, :], high[:, rest], preferred_element_type=F32)
-            hl[take, :] = jnp.dot(high[take, :], low[...], preferred_element_type=F32)
-            for j in (2 * p, 2 * p + 1):
-                for i in range(j + 1):
-                    use(i, j, hh[at(i), at(j)] + (hl[at(i), at(j)] + hl[at(j), at(i)].T))
+            cross = jnp.dot(high[take, :], low[:, rest], preferred_element_type=F32)
+            panel = jnp.dot(high[take, :], high[:, rest], preferred_element_type=F32) + cross
+            if p < NB // 2 - 1:
+                after = slice((p + 1) * step, width)
+                other = jnp.dot(low[take, :], high[:, after], preferred_element_type=F32)
+            for i in (2 * p, 2 * p + 1):
+                for j in range(i, NB):
+                    r, c = at(i - 2 * p), at(j - 2 * p)
+                    if j < 2 * p + 2:
+                        value = panel[r, c] + cross[c, r].T
+                    else:
+                        value = panel[r, c] + other[r, at(j - 2 * p - 2)]
+                    use(i, j, value)
 
     trace = jnp.sum(trace, axis=(0, 1), keepdims=True)
     square = jnp.sum(square, axis=(0, 1), keepdims=True)
@@ -382,14 +401,14 @@
     ).astype(BF16)
     load.wait()
     stores = []
-    for k in range(width // step):
-        cols = slice(k * step, (k + 1) * step)
+    for k, (first, size) in enumerate(CHUNKS):
+        cols = slice(first, first + size)
         value = jnp.dot(x_ref[...], bh[:, cols], preferred_element_type=F32) + jnp.dot(
             x_ref[...], bl[:, cols], preferred_element_type=F32
         )
         shift = jnp.sum(value[n_rows:, :], axis=0, keepdims=True)
         o_ref[:, cols] = (value[:n_rows, :] - shift).astype(BF16)
-        cols = pl.ds(k * step, step)
+        cols = pl.ds(first, size)
         store = pltpu.make_async_copy(o_ref.at[:, cols], o_hbm.at[:, cols], store_sem.at[k])
         store.start()
         stores.append(store)
@@ -407,9 +426,9 @@
         in_specs=[pl.BlockSpec(memory_space=pltpu.VMEM), hbm],
         out_specs=hbm,
         scratch_shapes=[pltpu.VMEM((x.shape[0] + 16, width), BF16), pltpu.VMEM(x.shape, BF16)]
-        + [pltpu.VMEM((width, width), F32)] * 3
+        + [pltpu.VMEM((width, width), F32)]
         + [pltpu.VMEM((width, width), BF16)] * 4
-        + [pltpu.SemaphoreType.DMA, pltpu.SemaphoreType.DMA((width // (2 * BLK),))],
+        + [pltpu.SemaphoreType.DMA, pltpu.SemaphoreType.DMA((len(CHUNKS),))],
         compiler_params=pltpu.CompilerParams(vmem_limit_bytes=48 * 2**20),
     )(pooled, x)
 

time: 65.9 us -> 65.7 us (level)
  no operation moved by 1% of the time
where the time goes in v5:
time: 65.7 us; the launch traced here: 65.6 us
  Pallas kernels  65.6 us (100%)
    pallas_call x1, Pallas kernels, pool(): pl.pallas_call(pool_kernel, name='pool', out_shape=jax.ShapeDtypeStruct((...  52.9 us
    pallas_call x1, Pallas kernels, white(): pl.pallas_call(white_kernel, name='white', out_shape=jax.ShapeDtypeStruct...  12.6 us

profile of v5, /device:TPU:1, one launch (start us, length us, event | category | flops | bytes accessed | tf_op | source)
XLA Modules:
  0.0 65.6 jit_solution(15292649032889814780)
XLA Ops:
  0.0 52.9 %pool.1.f_ref = f32[2,2568,128]{2,1,0:T(8,128)S(1)} custom-call(bf16[512,1024]{1,0:T(8,128)(2,1)} %x_hbm.3, s32[1,512]{1,0:T(1,128)} %bitcast.1), custom_call_target="tpu_custom_call" | custom-call | tf_op jit(solution)/shard_map/pool/pallas_call | solution.py:273
  53.0 12.6 %white.1 = bf16[512,1024]{1,0:T(8,128)(2,1)} custom-call(f32[2,2568,128]{2,1,0:T(8,128)S(1)} %pool.1.f_ref, bf16[512,1024]{1,0:T(8,128)(2,1)} %x_hbm.3), custom_call_target="tpu_custom_call" | custom-call | tf_op jit(solution)/shard_map/white/pallas_call | solution.py:422

commit v6 on v5

--- a/solution.py
+++ b/solution.py
@@ -306,7 +306,6 @@
     load = pltpu.make_async_copy(x_hbm, x_ref.at[pl.ds(0, n_rows)], load_sem)
     load.start()
     count = f_ref[1, D0:D0 + 1, :]
-    inverse = 1.0 / count
     sums = f_ref[0, D0:D0 + 8, :]
     center = sums / count
     diag = (
@@ -323,12 +322,12 @@
         high[at(i), at(j)] = h
         low[at(i), at(j)] = l
         if i != j:
-            h, l = split(value.T)
-            high[at(j), at(i)] = h
-            low[at(j), at(i)] = l
+            high[at(j), at(i)] = h.T
+            low[at(j), at(i)] = l.T
 
     trace = jnp.zeros((BLK, BLK), F32)
-    square = jnp.zeros((BLK, BLK), F32)
+    on_diag = jnp.zeros((BLK, BLK), F32)
+    off_diag = jnp.zeros((BLK, BLK), F32)
     for i in range(NB):
         column = jnp.broadcast_to(sums[i:i + 1, :], (BLK, BLK)).T
         for j in range(i, NB):
@@ -337,14 +336,13 @@
                 [f_ref[half, to:to + n, :] for _, to, n in runs(row, result_row)], axis=0
             )
             scatter = pooled - column * center[j:j + 1, :]
-            cov = scatter * inverse
             if i == j:
-                trace = trace + jnp.where(diag, cov, 0.0)
-                square = square + cov * cov
+                trace = trace + jnp.where(diag, scatter, 0.0)
+                on_diag = on_diag + scatter * scatter
             else:
-                square = square + 2.0 * (cov * cov)
-            b[at(i), at(j)] = cov
-            put(cov, i, j, bh, bl)
+                off_diag = off_diag + scatter * scatter
+            b[at(i), at(j)] = scatter
+            put(scatter, i, j, bh, bl)
 
     step = 2 * BLK
 
@@ -365,27 +363,32 @@
                         value = panel[r, c] + other[r, at(j - 2 * p - 2)]
                     use(i, j, value)
 
-    trace = jnp.sum(trace, axis=(0, 1), keepdims=True)
-    square = jnp.sum(square, axis=(0, 1), keepdims=True)
+    inverse = 1.0 / count[:, 0:1]
+    trace = jnp.sum(trace, axis=(0, 1), keepdims=True) * inverse
+    square = jnp.sum(on_diag + 2.0 * off_diag, axis=(0, 1), keepdims=True) * inverse * inverse
     ridge = 0.05 * trace / width + 1e-06
     norm = jnp.sqrt(square + 2.0 * ridge * trace + width * ridge * ridge)
     inv_norm = 1.0 / norm
-    inv_norm2 = inv_norm * inv_norm
     scale = lax.rsqrt(norm) / 16.0
+    part = jnp.sqrt(scale)
+
+    base = (0.0 * inv_norm, inverse * inv_norm, ridge * inv_norm)
+    base2 = (base[1] * base[1], 2.0 * base[1] * base[2], base[2] * base[2])
+    s_of = [part * (two - 4.5 * one) for two, one in zip(base2, base)]
+    rest_of = [scale * (6.75 * two - 39.0 * one) for two, one in zip(base2, base)]
+    rest_of[2] = rest_of[2] + 36.0 * scale
 
     def half_way(i, j, value):
-        cov = b[at(i), at(j)]
-        value = value + (2.0 * ridge) * cov
+        own = b[at(i), at(j)]
+        s = s_of[0] * value + s_of[1] * own
+        rest = rest_of[0] * value + rest_of[1] * own
         if i == j:
-            value = value + (ridge * ridge) * eye
-            cov = cov + ridge * eye
-        base, base2 = cov * inv_norm, value * inv_norm2
-        put(base2 - 4.5 * base, i, j, sh, sl)
-        rest = 6.75 * base2 - 39.0 * base
-        b[at(i), at(j)] = rest + 36.0 * eye if i == j else rest
+            s, rest = s + s_of[2] * eye, rest + rest_of[2] * eye
+        put(s, i, j, sh, sl)
+        b[at(i), at(j)] = rest
 
     def rooted(i, j, value):
-        put((value + b[at(i), at(j)]) * scale, i, j, bh, bl)
+        put(value + b[at(i), at(j)], i, j, bh, bl)
 
     squared(bh, bl, half_way)
     squared(sh, sl, rooted)

time: 65.7 us -> 65.1 us (level)
  Pallas kernels: 65.6 us -> 64.9 us
where the time goes in v6:
time: 65.1 us; the launch traced here: 64.9 us
  Pallas kernels  64.9 us (100%)
    pallas_call x1, Pallas kernels, pool(): pl.pallas_call(pool_kernel, name='pool', out_shape=jax.ShapeDtypeStruct((...  52.9 us
    pallas_call x1, Pallas kernels, white(): pl.pallas_call(white_kernel, name='white', out_shape=jax.ShapeDtypeStruct...  12 us

profile of v6, /device:TPU:1, one launch (start us, length us, event | category | flops | bytes accessed | tf_op | source)
XLA Modules:
  0.0 64.9 jit_solution(8237330760299926611)
XLA Ops:
  0.0 52.9 %pool.1.f_ref = f32[2,2568,128]{2,1,0:T(8,128)S(1)} custom-call(bf16[512,1024]{1,0:T(8,128)(2,1)} %x_hbm.3, s32[1,512]{1,0:T(1,128)} %bitcast.1), custom_call_target="tpu_custom_call" | custom-call | tf_op jit(solution)/shard_map/pool/pallas_call | solution.py:273
  53.0 12.0 %white.1 = bf16[512,1024]{1,0:T(8,128)(2,1)} custom-call(f32[2,2568,128]{2,1,0:T(8,128)S(1)} %pool.1.f_ref, bf16[512,1024]{1,0:T(8,128)(2,1)} %x_hbm.3), custom_call_target="tpu_custom_call" | custom-call | tf_op jit(solution)/shard_map/white/pallas_call | solution.py:425

commit v7 on v6

--- a/solution.py
+++ b/solution.py
@@ -166,8 +166,8 @@
     def beside(axis, step):
         return moved(me, axis, step)[axis]
 
-    cuts = [pl.ds(GB, 8 * BY), pl.ds(GC, 8 * BY)]
-    cuts += [rows(GX * beside("x", s), GX) for s in FAR_4 + (0,)]
+    cuts = [pl.ds(GB, 8 * BY), rows(GX * beside("x", 2), GX), pl.ds(GC, 8 * BY)]
+    cuts += [rows(GX * beside("x", s), GX) for s in (1, 3, 0)]
     pair = [copy(g.at[1 - core, cut], got.at[cut], "c", 1) for cut in cuts]
 
     def add_pair(k):
@@ -176,12 +176,14 @@
 
     add_pair(0)
     w1y = [copy(acc.at[rows(GB + BY * beside("y", s), BY)], r1y.at[s - 1], "y", s) for s in FAR_8]
+    w1x = []
     add_pair(1)
+    w1x.append(copy(acc.at[cuts[1]], r1x.at[1], "x", 2))
+    add_pair(2)
     w1z = [copy(acc.at[rows(GC + BY * beside("z", s), BY)], r1z.at[s - 1], "z", s) for s in FAR_8]
-    w1x = []
-    for k, s in enumerate(FAR_4):
-        add_pair(k + 2)
-        w1x.append(copy(acc.at[cuts[k + 2]], r1x.at[s - 1], "x", s))
+    for k, s in ((3, 1), (4, 3)):
+        add_pair(k)
+        w1x.append(copy(acc.at[cuts[k]], r1x.at[s - 1], "x", s))
     add_pair(5)
 
     def quarters(value, first):
@@ -292,9 +294,6 @@
     )(x, valid)
 
 
-CHUNKS = ((0, 512), (512, 256), (768, 256))
-
-
 def split(value):
     high = value.astype(BF16)
     return high, (value - high.astype(F32)).astype(BF16)
@@ -403,20 +402,24 @@
         jnp.where(which == 1, c_mid, jnp.where(which == 2, c_low, 0.0)),
     ).astype(BF16)
     load.wait()
-    stores = []
-    for k, (first, size) in enumerate(CHUNKS):
-        cols = slice(first, first + size)
+
+    def store(k):
+        cols = pl.ds(pl.multiple_of(k * step, step), step)
+        return pltpu.make_async_copy(o_ref.at[:, cols], o_hbm.at[:, cols], store_sem.at[k])
+
+    @pl.loop(0, width // step)
+    def _(k):
+        cols = pl.ds(pl.multiple_of(k * step, step), step)
         value = jnp.dot(x_ref[...], bh[:, cols], preferred_element_type=F32) + jnp.dot(
             x_ref[...], bl[:, cols], preferred_element_type=F32
         )
         shift = jnp.sum(value[n_rows:, :], axis=0, keepdims=True)
         o_ref[:, cols] = (value[:n_rows, :] - shift).astype(BF16)
-        cols = pl.ds(first, size)
-        store = pltpu.make_async_copy(o_ref.at[:, cols], o_hbm.at[:, cols], store_sem.at[k])
-        store.start()
-        stores.append(store)
-    for store in stores:
-        store.wait()
+        store(k).start()
+
+    @pl.loop(0, width // step)
+    def _(k):
+        store(k).wait()
 
 
 def white(pooled, x):
@@ -431,7 +434,7 @@
         scratch_shapes=[pltpu.VMEM((x.shape[0] + 16, width), BF16), pltpu.VMEM(x.shape, BF16)]
         + [pltpu.VMEM((width, width), F32)]
         + [pltpu.VMEM((width, width), BF16)] * 4
-        + [pltpu.SemaphoreType.DMA, pltpu.SemaphoreType.DMA((len(CHUNKS),))],
+        + [pltpu.SemaphoreType.DMA, pltpu.SemaphoreType.DMA((width // (2 * BLK),))],
         compiler_params=pltpu.CompilerParams(vmem_limit_bytes=48 * 2**20),
     )(pooled, x)
 

time: 65.1 us -> 65.4 us (level)
  no operation moved by 1% of the time
where the time goes in v7:
time: 65.4 us; the launch traced here: 65.3 us
  Pallas kernels  65.3 us (100%)
    pallas_call x1, Pallas kernels, pool(): pl.pallas_call(pool_kernel, name='pool', out_shape=jax.ShapeDtypeStruct((...  52.7 us
    pallas_call x1, Pallas kernels, white(): pl.pallas_call(white_kernel, name='white', out_shape=jax.ShapeDtypeStruct...  12.5 us

profile of v7, /device:TPU:1, one launch (start us, length us, event | category | flops | bytes accessed | tf_op | source)
XLA Modules:
  0.0 65.3 jit_solution(13836692648250609970)
XLA Ops:
  0.0 52.7 %pool.1.f_ref = f32[2,2568,128]{2,1,0:T(8,128)S(1)} custom-call(bf16[512,1024]{1,0:T(8,128)(2,1)} %x_hbm.3, s32[1,512]{1,0:T(1,128)} %bitcast.1), custom_call_target="tpu_custom_call" | custom-call | tf_op jit(solution)/shard_map/pool/pallas_call | solution.py:275
  52.7 12.5 %white.1 = bf16[512,1024]{1,0:T(8,128)(2,1)} custom-call(f32[2,2568,128]{2,1,0:T(8,128)S(1)} %pool.1.f_ref, bf16[512,1024]{1,0:T(8,128)(2,1)} %x_hbm.3), custom_call_target="tpu_custom_call" | custom-call | tf_op jit(solution)/shard_map/white/pallas_call | solution.py:428

commit v8 on v6

--- a/solution.py
+++ b/solution.py
@@ -166,8 +166,8 @@
     def beside(axis, step):
         return moved(me, axis, step)[axis]
 
-    cuts = [pl.ds(GB, 8 * BY), pl.ds(GC, 8 * BY)]
-    cuts += [rows(GX * beside("x", s), GX) for s in FAR_4 + (0,)]
+    cuts = [pl.ds(GB, 8 * BY), rows(GX * beside("x", 2), GX), pl.ds(GC, 8 * BY)]
+    cuts += [rows(GX * beside("x", s), GX) for s in (1, 3, 0)]
     pair = [copy(g.at[1 - core, cut], got.at[cut], "c", 1) for cut in cuts]
 
     def add_pair(k):
@@ -176,12 +176,14 @@
 
     add_pair(0)
     w1y = [copy(acc.at[rows(GB + BY * beside("y", s), BY)], r1y.at[s - 1], "y", s) for s in FAR_8]
+    w1x = []
     add_pair(1)
+    w1x.append(copy(acc.at[cuts[1]], r1x.at[1], "x", 2))
+    add_pair(2)
     w1z = [copy(acc.at[rows(GC + BY * beside("z", s), BY)], r1z.at[s - 1], "z", s) for s in FAR_8]
-    w1x = []
-    for k, s in enumerate(FAR_4):
-        add_pair(k + 2)
-        w1x.append(copy(acc.at[cuts[k + 2]], r1x.at[s - 1], "x", s))
+    for k, s in ((3, 1), (4, 3)):
+        add_pair(k)
+        w1x.append(copy(acc.at[cuts[k]], r1x.at[s - 1], "x", s))
     add_pair(5)
 
     def quarters(value, first):

time: 65.1 us -> 64.8 us (level)
  no operation moved by 1% of the time
where the time goes in v8:
time: 64.8 us; the launch traced here: 64.7 us
  Pallas kernels  64.7 us (100%)
    pallas_call x1, Pallas kernels, pool(): pl.pallas_call(pool_kernel, name='pool', out_shape=jax.ShapeDtypeStruct((...  52.7 us
    pallas_call x1, Pallas kernels, white(): pl.pallas_call(white_kernel, name='white', out_shape=jax.ShapeDtypeStruct...  12 us

profile of v8, /device:TPU:1, one launch (start us, length us, event | category | flops | bytes accessed | tf_op | source)
XLA Modules:
  0.0 64.7 jit_solution(1149416567001778049)
XLA Ops:
  0.0 52.7 %pool.1.f_ref = f32[2,2568,128]{2,1,0:T(8,128)S(1)} custom-call(bf16[512,1024]{1,0:T(8,128)(2,1)} %x_hbm.3, s32[1,512]{1,0:T(1,128)} %bitcast.1), custom_call_target="tpu_custom_call" | custom-call | tf_op jit(solution)/shard_map/pool/pallas_call | solution.py:275
  52.7 12.0 %white.1 = bf16[512,1024]{1,0:T(8,128)(2,1)} custom-call(f32[2,2568,128]{2,1,0:T(8,128)S(1)} %pool.1.f_ref, bf16[512,1024]{1,0:T(8,128)(2,1)} %x_hbm.3), custom_call_target="tpu_custom_call" | custom-call | tf_op jit(solution)/shard_map/white/pallas_call | solution.py:427
